TPU v7x, 256 devices: a whole 4x4x8 slice. The times are simulated.
256 devices in a mesh: gx: 16 (over y, x), gy: 16 (over z, core).
Axes of the slice: x: 4, y: 4, z: 8, core: 2. Of those that a mesh axis runs over, the one named last changes fastest.
Arguments:
- pressure: float32 [2, 2048, 2048], P(None, 'gx', 'gy'), may hold values from 0.5 to 1.5
- saturations: float32 [2, 2, 2048, 2048], P(None, None, 'gx', 'gy'), may hold values from 0.05 to 0.4
- old_mass: float32 [3, 2, 2048, 2048], P(None, None, 'gx', 'gy'), may hold values from 0 to 0.4
- pore_volume: float32 [2, 2048, 2048], P(None, 'gx', 'gy'), may hold values from 0.3 to 3
- transmissibility: float32 [3, 2, 2048, 2048], P(None, None, 'gx', 'gy'), may hold values from 0.3 to 3
- direction: float32 [3, 2, 2048, 2048], P(None, None, 'gx', 'gy'), may hold values from -6 to 6
- seg_pressure: float32 [512, 128], P('gx'), may hold values from 0.4 to 1.2
- seg_direction: float32 [512, 128], P('gx'), may hold values from -6 to 6
- perf_cell: int32 [512, 128], P('gx'), may hold values from 0 to 524287, as said below
- well_index: float32 [512, 128], P('gx'), may hold values from 0.2 to 2
- parent: int32 [512, 128], P('gx'), may hold values from 0 to 126, as said below
- seg_head: float32 [512, 128], P('gx'), may hold values from 0 to 0.3
- well_mode: int32 [512], P('gx'), may hold values from 0 to 1
- bhp_limit: float32 [512], P('gx'), may hold values from 0.3 to 0.8
- guide_rate: float32 [512], P('gx'), may hold values from 0.5 to 5
- group_of: int32 [512, 1], P('gx'), may hold values from 0 to 127
- group_target: float32 [128], replicated, may hold values from 200 to 800
Outputs:
- cell_residual: float32 [3, 2, 2048, 2048], P(None, None, 'gx', 'gy')
- cell_jvp: float32 [3, 2, 2048, 2048], P(None, None, 'gx', 'gy')
- seg_residual: float32 [512, 128], P(('gx', 'gy'))
- seg_jvp: float32 [512, 128], P(('gx', 'gy'))
- group_rates: float32 [3, 128], replicated
Inputs may be any that keep to these rules, and one draw needn't show every extreme that they name: perf_cell codes (layer * 128 + xl) * 2048 + row, with xl the column within the strip of 128 columns of the well's block of 32 wells. `parent`: segment 0 of every well names itself; every other segment names a segment of lower number. `group_of`: every group has at least one well.
All inputs are finite; a program needn't handle non-finite values.
Results may differ from a plain program's by a relative error of at most 0.0003.
Values sent between devices are 32-bit elements; how exact they have to be, the bound alone decides.
A program may use at most 128 MiB of HBM per device.

v0:
```python
import jax
import jax.numpy as jnp
from jax import lax
from jax.sharding import PartitionSpec as P

COMPRESS = (0.05, 0.2, 1.0)
VISCOSITY = (0.5, 1.0, 0.2)
DENSITY = (1.0, 0.8, 0.2)
ROCK_COMP = 0.01
GRAVITY = 0.05
UPWIND_WIDTH = 0.02
FRICTION = 0.002
RATE_SCALE = 0.1


def padded_2(x, sides, width):
    for axis, dim in sides:
        devices, length = (lax.axis_size(axis), x.shape[dim])
        up = [(i, (i + 1) % devices) for i in range(devices - 1)]
        down = [(j, i) for i, j in up]
        last = lax.slice_in_dim(x, length - width, length, axis=dim)
        first = lax.slice_in_dim(x, 0, width, axis=dim)
        before = lax.ppermute(last, axis, up)
        after = lax.ppermute(first, axis, down)
        x = jnp.concatenate([before, x, after], axis=dim)
    return x


def phase_props(press, water, gas):
    oil = 1.0 - water - gas
    satur = (water, oil, gas)
    rock = 1.0 + ROCK_COMP * (press - 1.0)
    mobility = []
    masses = []
    for phase in range(3):
        volume = jnp.exp(COMPRESS[phase] * (press - 1.0))
        mobility.append(satur[phase] * satur[phase] * volume / VISCOSITY[phase])
        masses.append(rock * satur[phase] * volume)
    return (jnp.stack(mobility), jnp.stack(masses))


def face_flux(press_in, press_out, mobil_in, mobil_out, trans, lift):
    fluxes = []
    for phase in range(3):
        potential = press_in - press_out + DENSITY[phase] * lift
        upwind = jax.nn.sigmoid(potential / UPWIND_WIDTH)
        fluxes.append(
            trans * (upwind * mobil_in[phase] + (1.0 - upwind) * mobil_out[phase]) * potential
        )
    return jnp.stack(fluxes)


def ancestry(parent):
    count = parent.shape[1]
    segment_ids = jnp.arange(count, dtype=jnp.int32)
    reach = (segment_ids[None, :, None] == segment_ids[None, None, :]) | (
        parent[:, None, :] == segment_ids[None, :, None]
    )
    reach = reach.astype(jnp.bfloat16)
    for level in range((count - 1).bit_length()):
        product = jnp.einsum("wsu,wut->wst", reach, reach, preferred_element_type=jnp.float32)
        reach = jnp.minimum(product, 1.0).astype(jnp.bfloat16)
    return reach.astype(jnp.float32)


def segment_terms(parent, seg_head, well_mode, bhp_limit, target):
    reach = ancestry(parent)

    def equations(total_vals, seg_vals):
        flow = jnp.einsum("wst,wt->ws", reach, total_vals, precision=lax.Precision.HIGHEST)
        above = jnp.take_along_axis(seg_vals, parent, axis=1)
        inner = seg_vals - above - seg_head - FRICTION * flow
        root = jnp.where(
            well_mode == 1, RATE_SCALE * (flow[:, 0] - target), seg_vals[:, 0] - bhp_limit
        )
        return inner.at[:, 0].set(root)

    return equations


def per_device(
    pressure,
    saturations,
    old_mass,
    pore_volume,
    transmissibility,
    direction,
    seg_pressure,
    seg_direction,
    perf_cell,
    well_index,
    parent,
    seg_head,
    well_mode,
    bhp_limit,
    guide_rate,
    group_of,
    group_target,
):
    layers, cols, rows = pressure.shape
    col_count = lax.axis_size("gx")
    row_count = lax.axis_size("gy")
    col_index = lax.axis_index("gx")
    row_index = lax.axis_index("gy")
    col_glob = col_index * cols + jnp.arange(cols, dtype=jnp.int32)
    row_glob = row_index * rows + jnp.arange(rows, dtype=jnp.int32)
    trans_cols = jnp.where(
        (col_glob == cols * col_count - 1)[None, :, None], 0.0, transmissibility[0]
    )
    trans_rows = jnp.where(
        (row_glob == rows * row_count - 1)[None, None, :], 0.0, transmissibility[1]
    )
    stacked = jnp.concatenate(
        [pressure[None], saturations, direction, trans_cols[None], trans_rows[None]], axis=0
    )
    padded = padded_2(stacked, (("gx", 2), ("gy", 3)), 1)
    state_pad = padded[0:3]
    direc_pad = padded[3:6]
    tcol_pad = padded[6]
    trow_pad = padded[7]
    all_rows = rows * row_count
    layer_span = cols * all_rows
    layer = perf_cell // layer_span
    remain = perf_cell % layer_span
    local_row = remain % all_rows - row_index * rows
    owned = (local_row >= 0) & (local_row < rows)
    flat_cell = (layer * cols + remain // all_rows) * rows + jnp.clip(local_row, 0, rows - 1)
    weight = jnp.where(owned, well_index, 0.0)

    def local_terms(state, seg_vals):
        press = state[0]
        mobility, masses = phase_props(press, state[1], state[2])
        mobil_in = mobility[:, :, 1:-1, 1:-1]
        press_in = press[:, 1:-1, 1:-1]
        residual = masses[:, :, 1:-1, 1:-1] * pore_volume - old_mass
        flux_cols = face_flux(
            press[:, :-1, 1:-1],
            press[:, 1:, 1:-1],
            mobility[:, :, :-1, 1:-1],
            mobility[:, :, 1:, 1:-1],
            tcol_pad[:, :-1, 1:-1],
            0.0,
        )
        residual = residual + flux_cols[:, :, 1:] - flux_cols[:, :, :-1]
        flux_rows = face_flux(
            press[:, 1:-1, :-1],
            press[:, 1:-1, 1:],
            mobility[:, :, 1:-1, :-1],
            mobility[:, :, 1:-1, 1:],
            trow_pad[:, 1:-1, :-1],
            0.0,
        )
        residual = residual + flux_rows[:, :, :, 1:] - flux_rows[:, :, :, :-1]
        flux_layers = face_flux(
            press_in[:-1],
            press_in[1:],
            mobil_in[:, :-1],
            mobil_in[:, 1:],
            transmissibility[2][:-1],
            GRAVITY,
        )
        residual = (
            residual
            + jnp.pad(flux_layers, ((0, 0), (0, 1), (0, 0), (0, 0)))
            - jnp.pad(flux_layers, ((0, 0), (1, 0), (0, 0), (0, 0)))
        )
        mobil_flat = mobil_in.reshape(3, -1)
        rates = weight * mobil_flat[:, flat_cell] * (press_in.reshape(-1)[flat_cell] - seg_vals)
        residual = (
            residual.reshape(3, -1)
            .at[:, flat_cell.reshape(-1)]
            .add(rates.reshape(3, -1))
            .reshape(residual.shape)
        )
        return (residual, rates)

    primal, tangent = jax.jvp(local_terms, (state_pad, seg_pressure), (direc_pad, seg_direction))
    cell_residual, rates = primal
    cell_jvp, rate_tangent = tangent
    rate_total = jnp.sum(rates, axis=0)
    total_tangent = jnp.sum(rate_tangent, axis=0)
    member = (
        group_of[:, 0][:, None] == jnp.arange(group_target.shape[0], dtype=jnp.int32)[None, :]
    ).astype(jnp.float32)
    rates_part = jnp.dot(jnp.sum(rates, axis=2), member, precision=lax.Precision.HIGHEST)
    guide_part = jnp.dot(guide_rate, member, precision=lax.Precision.HIGHEST)
    guide_total = lax.psum(guide_part, "gx")
    group_rates = lax.psum(rates_part, ("gx", "gy"))
    target = (
        jnp.dot(member, group_target, precision=lax.Precision.HIGHEST)
        * guide_rate
        / jnp.dot(member, guide_total, precision=lax.Precision.HIGHEST)
    )
    well_count = seg_pressure.shape[0]
    share = well_count // row_count
    start = row_index * share

    def pick(values):
        return lax.dynamic_slice_in_dim(values, start, share, 0)

    total_sum, tangent_sum = lax.psum((rate_total, total_tangent), "gy")
    equations = segment_terms(parent, seg_head, well_mode, bhp_limit, target)
    seg_full, seg_tan = jax.jvp(equations, (total_sum, seg_pressure), (tangent_sum, seg_direction))
    seg_residual = pick(seg_full)
    seg_jvp = pick(seg_tan)
    return (cell_residual, cell_jvp, seg_residual, seg_jvp, group_rates)


def solution(mesh):
    placed = (
        P(None, "gx", "gy"),
        P(None, None, "gx", "gy"),
        P(None, None, "gx", "gy"),
        P(None, "gx", "gy"),
        P(None, None, "gx", "gy"),
        P(None, None, "gx", "gy"),
        P("gx", None),
        P("gx", None),
        P("gx", None),
        P("gx", None),
        P("gx", None),
        P("gx", None),
        P("gx"),
        P("gx"),
        P("gx"),
        P("gx", None),
        P(),
    )
    return jax.shard_map(
        per_device,
        mesh=mesh,
        in_specs=placed,
        out_specs=(
            P(None, None, "gx", "gy"),
            P(None, None, "gx", "gy"),
            P(("gx", "gy"), None),
            P(("gx", "gy"), None),
            P(),
        ),
        check_vma=False,
    )
```

profile of v0, /device:TPU:1, one launch (start us, length us, event | category | flops | bytes accessed | tf_op | source)
XLA Modules:
  0.0 510.7 jit_solution(14686973665699037031)
XLA Ops:
  0.7 0.9 bitcast_dynamic-update-slice_fusion
  1.7 1.0 constant_dynamic-update-slice_fusion.1
  2.6 1.0 constant_dynamic-update-slice_fusion
  3.7 1.0 select_dynamic-update-slice_fusion.1
  4.7 0.9 select_dynamic-update-slice_fusion
  5.6 1.3 collective-permute-start.1
  6.9 4.6 collective-permute-start
  11.6 0.6 compare_select_fusion
  12.2 0.8 minimum_convert_fusion.6
  13.0 1.0 minimum_convert_fusion.4
  14.0 1.0 minimum_convert_fusion.2
  15.0 2.0 minimum_convert_fusion
  17.2 32.3 %psum.29 = f32[128]{0:T(128)S(1)} all-reduce(f32[128]{0:T(128)S(1)} %convolution_bitcast_fusion.1), channel_id=1, replica_groups=mesh['gx'=16,'gy'=16] {'gx'}, use_global_device_ids=true, to_apply=%region_5.6 | all-reduce | flops 128 | bytes 1024 | tf_op jit(solution)/shard_map/psum | solution.py:187
  49.5 0.7 convolution_bitcast_fusion
  50.2 0.6 slice_reduce_fusion.2
  50.9 0.4 fusion.172
  51.3 0.6 copy.106
  51.9 9.9 %collective-permute-start.3 = (f32[8,2,130,1]{2,0,3,1:T(8,128)S(1)}, f32[8,2,130,1]{2,0,3,1:T(8,128)S(1)}, u32[]{:S(2)}, u32[]{:S(2)}) collective-permute-start(f32[8,2,130,1]{2,0,3,1:T(8,128)S(1)} %copy.106), channel_id=1, source_target_pairs={{1,0},{2,1},{3,2},{4,3},{5,4},{6,5},{7,6},{8,7},{9,8},{10,9},{11,1... | collective-permute-start | bytes 24968 | tf_op jit(solution)/shard_map/ppermute | solution.py:24
  61.8 0.6 copy.105
  62.4 3.6 collective-permute-start.2
  66.2 43.2 %gather_fusion.5 = f32[4096]{0:T(1024)} fusion(f32[32,128]{1,0:T(8,128)S(1)} %copy-done.1, s32[4096]{0:T(1024)S(1)} %fusion.156), kind=kCustom, calls=%fused_computation.5 | custom fusion | bytes 65536 | tf_op jit(solution)/shard_map/jvp(jit(take_along_axis))/gather | solution.py:71
  109.4 25.6 %gather_fusion.4 = f32[4096]{0:T(1024)S(1)} fusion(f32[32,128]{1,0:T(8,128)S(1)} %copy-done.2, s32[4096]{0:T(1024)S(1)} %fusion.156), kind=kCustom, calls=%fused_computation.4 | custom fusion | bytes 65536 | tf_op jit(solution)/shard_map/jvp(jit(take_along_axis))/gather | solution.py:71
  135.0 0.6 compare_reduce_fusion
  135.7 0.4 copy.108
  136.1 0.4 copy.107
  136.5 1.0 pad_maximum_fusion
  137.6 0.3 fusion.38
  138.1 1.2 fusion.39
  139.3 0.5 fusion.54
  139.8 0.4 fusion.89
  140.2 0.3 multiply_bitcast_fusion.2
  140.5 0.2 multiply_bitcast_fusion.5
  140.7 0.7 fusion.60
  141.4 0.5 fusion.95
  141.9 0.2 fusion.118
  142.1 0.3 fusion.127
  142.5 0.3 pad_maximum_fusion.6
  143.0 1.0 pad_maximum_fusion.2
  144.1 0.7 pad_maximum_fusion.14
  144.8 0.3 fusion.34
  145.2 8.6 %copy.109 = f32[3,2,128,128]{0,3,2,1:T(8,128)} copy(f32[3,2,128,128]{3,2,1,0:T(8,128)S(1)} %fusion.34) | data formatting | bytes 786432 | tf_op jit(solution)/shard_map/jvp()/sub | solution.py:163
  153.7 8.5 %copy.110 = f32[3,2,128,128]{0,3,2,1:T(8,128)} copy(f32[3,2,128,128]{3,2,1,0:T(8,128)S(1)} %get-tuple-element.106) | data formatting | bytes 786432 | tf_op jit(solution)/shard_map/jvp()/slice | solution.py:133
  162.2 16.5 %gather_fusion = f32[4096,3]{1,0:T(8,128)S(1)} fusion(f32[3,32768]{0,1:T(8,128)} %bitcast.414, s32[4096]{0:T(1024)S(1)} %get-tuple-element.69), kind=kCustom, calls=%fused_computation | custom fusion | bytes 114688 | tf_op jit(solution)/shard_map/jvp()/gather | solution.py:168
  178.8 40.6 %gather_fusion.3 = f32[4096]{0:T(1024)} fusion(f32[32768]{0:T(1024)S(1)} %bitcast.407, s32[4096]{0:T(1024)S(1)} %get-tuple-element.69), kind=kCustom, calls=%fused_computation.3 | custom fusion | bytes 49152 | tf_op jit(solution)/shard_map/jvp()/gather | solution.py:168
  219.4 23.0 %gather_fusion.1 = f32[4096]{0:T(1024)S(1)} fusion(f32[32768]{0:T(1024)S(1)} %bitcast.408, s32[4096]{0:T(1024)S(1)} %get-tuple-element.69), kind=kCustom, calls=%fused_computation.1 | custom fusion | bytes 49152 | tf_op jit(solution)/shard_map/jvp()/gather | solution.py:168
  242.4 36.5 %scatter_custom_fusion = f32[3,32768]{0,1:T(8,128)} fusion(f32[3,32768]{0,1:T(8,128)} %bitcast.409, s32[4096]{0:T(1024)} %bitcast.429, f32[4096,3]{1,0:T(8,128)S(1)} %gather_fusion, f32[4096]{0:T(1024)S(1)} %bitcast.419, f32[4096]{0:T(1024)S(1)} %bitcast.417), kind=kCustom, calls=%fused_computation.15 | custom fusion | flops 36864 | bytes 475136 | tf_op jit(solution)/shard_map/jvp()/scatter-add | solution.py:172
  278.9 10.7 %copy.115 = f32[3,2,128,128]{3,2,1,0:T(8,128)} copy(f32[3,2,128,128]{0,3,2,1:T(8,128)} %bitcast.410) | data formatting | bytes 786432
  289.6 2.5 fusion.31
  292.1 9.5 %copy.111 = f32[3,2,128,128]{0,3,2,1:T(8,128)} copy(f32[3,2,128,128]{3,2,1,0:T(8,128)} %fusion.31) | data formatting | bytes 786432 | tf_op jit(solution)/shard_map/jvp()/sub | solution.py:163
  301.6 8.5 %copy.112 = f32[3,2,128,128]{0,3,2,1:T(8,128)} copy(f32[3,2,128,128]{3,2,1,0:T(8,128)S(1)} %get-tuple-element.105) | data formatting | bytes 786432 | tf_op jit(solution)/shard_map/jvp()/slice | solution.py:133
  310.1 19.9 %gather_fusion.2 = f32[4096,3]{1,0:T(8,128)} fusion(f32[3,32768]{0,1:T(8,128)} %bitcast.415, s32[4096]{0:T(1024)S(1)} %get-tuple-element.69), kind=kCustom, calls=%fused_computation.2 | custom fusion | bytes 114688 | tf_op jit(solution)/shard_map/jvp()/gather | solution.py:168
  330.1 37.0 %scatter_custom_fusion.1 = f32[3,32768]{0,1:T(8,128)} fusion(f32[3,32768]{0,1:T(8,128)} %bitcast.411, s32[4096]{0:T(1024)} %bitcast.430, f32[4096,3]{1,0:T(8,128)} %gather_fusion.2, f32[4096,3]{1,0:T(8,128)S(1)} %gather_fusion, f32[4096]{0:T(1024)S(1)} %bitcast.425, f32[4096]{0:T(1024)S(1)} %bitcast.420, f32[4096]{0:T(1024)S(1)} %bitcast.418), kind=kCustom, calls=%fused_computation.13 | custom fusion | flops 73728 | bytes 2588672 | tf_op jit(solution)/shard_map/jvp()/scatter-add | solution.py:172
  367.0 10.6 %copy.116 = f32[3,2,128,128]{3,2,1,0:T(8,128)} copy(f32[3,2,128,128]{0,3,2,1:T(8,128)} %bitcast.412) | data formatting | bytes 786432
  377.7 4.6 add_reduce_fusion
  382.4 46.0 %all-reduce.4 = (f32[32,128]{1,0:T(8,128)S(1)}, f32[32,128]{1,0:T(8,128)S(1)}) all-reduce(f32[32,128]{1,0:T(8,128)S(1)} %get-tuple-element.55, f32[32,128]{1,0:T(8,128)S(1)} %get-tuple-element.54), channel_id=1, replica_groups=mesh['gx'=16,'gy'=16] {'gy'}, use_global_device_ids=true, to_apply=%region_3.4 | all-reduce | flops 8192 | bytes 65536 | tf_op jit(solution)/shard_map/psum | solution.py:201
  428.4 1.7 fusion.175
  430.2 1.7 fusion.174
  432.2 0.2 fusion.19
  432.5 0.7 slice_select_fusion.1
  433.4 0.6 slice_select_fusion
  434.1 0.6 constant_dynamic-slice_fusion.1
  434.7 0.6 constant_dynamic-slice_fusion
  435.3 0.2 fusion.157
  435.5 75.3 %psum.31 = f32[3,128]{1,0:T(4,128)} all-reduce(f32[3,128]{1,0:T(4,128)S(1)} %fusion.157), channel_id=1, replica_groups=mesh['gx'=16,'gy'=16] {'gx','gy'}, use_global_device_ids=true, to_apply=%region_9.10 | all-reduce | flops 384 | bytes 3072 | tf_op jit(solution)/shard_map/psum | solution.py:188
  (73 shorter events, 1.9 us)
Async XLA Ops:
  0.6 431.5 %copy-start = (f32[128]{0:T(128)S(1)}, f32[128]{0:T(128)}, u32[]{:S(2)}) copy-start(f32[128]{0:T(128)} %param.37) | copy-start | bytes 1540
  0.6 10.9 %copy-start.8 = (s32[32,128]{1,0:T(8,128)S(1)}, s32[32,128]{1,0:T(8,128)}, u32[]{:S(2)}) copy-start(s32[32,128]{1,0:T(8,128)} %param.29) | copy-start | bytes 49156
  0.7 11.5 %copy-start.12 = (f32[32,128]{1,0:T(8,128)S(1)}, f32[32,128]{1,0:T(8,128)}, u32[]{:S(2)}) copy-start(f32[32,128]{1,0:T(8,128)} %param.30) | copy-start | bytes 49156
  0.7 11.5 %copy-start.9 = (s32[32,128]{1,0:T(8,128)S(1)}, s32[32,128]{1,0:T(8,128)}, u32[]{:S(2)}) copy-start(s32[32,128]{1,0:T(8,128)} %param.31) | copy-start | bytes 49156
  5.6 45.2 %collective-permute-start.1 = (f32[8,2,1,128]{3,2,1,0:T(1,128)S(1)}, f32[8,2,1,128]{3,2,1,0:T(1,128)S(1)}, u32[]{:S(2)}, u32[]{:S(2)}) collective-permute-start(f32[8,2,1,128]{3,2,1,0:T(1,128)S(1)} %get-tuple-element.89), channel_id=1, source_target_pairs={{16,0},{32,16},{48,32},{64,48},{80,64},{96,80},{112,96},{128,112},... | collective-permute-start | bytes 24584 | tf_op jit(solution)/shard_map/ppermute | solution.py:24
  6.9 43.9 %collective-permute-start = (f32[8,2,1,128]{3,2,1,0:T(1,128)S(1)}, f32[8,2,1,128]{3,2,1,0:T(1,128)S(1)}, u32[]{:S(2)}, u32[]{:S(2)}) collective-permute-start(f32[8,2,1,128]{3,2,1,0:T(1,128)S(1)} %get-tuple-element.88), channel_id=1, source_target_pairs={{0,16},{16,32},{32,48},{48,64},{64,80},{80,96},{96,112},{112,128},... | collective-permute-start | bytes 24584 | tf_op jit(solution)/shard_map/ppermute | solution.py:23
  15.0 2.0 copy-start.16
  15.0 2.0 copy-start.19
  15.0 35.2 %copy-start.2 = (f32[32,128]{1,0:T(8,128)S(1)}, f32[32,128]{1,0:T(8,128)}, u32[]{:S(2)}) copy-start(f32[32,128]{1,0:T(8,128)} %param.27) | copy-start | bytes 49156
  51.3 14.8 %copy-start.1 = (f32[32,128]{1,0:T(8,128)S(1)}, f32[32,128]{1,0:T(8,128)}, u32[]{:S(2)}) copy-start(f32[32,128]{1,0:T(8,128)} %param.28) | copy-start | bytes 49156
  51.9 83.8 %collective-permute-start.3 = (f32[8,2,130,1]{2,0,3,1:T(8,128)S(1)}, f32[8,2,130,1]{2,0,3,1:T(8,128)S(1)}, u32[]{:S(2)}, u32[]{:S(2)}) collective-permute-start(f32[8,2,130,1]{2,0,3,1:T(8,128)S(1)} %copy.106), channel_id=1, source_target_pairs={{1,0},{2,1},{3,2},{4,3},{5,4},{6,5},{7,6},{8,7},{9,8},{10,9},{11,1... | collective-permute-start | bytes 24968 | tf_op jit(solution)/shard_map/ppermute | solution.py:24
  62.4 73.7 %collective-permute-start.2 = (f32[8,2,130,1]{2,0,3,1:T(8,128)S(1)}, f32[8,2,130,1]{2,0,3,1:T(8,128)S(1)}, u32[]{:S(2)}, u32[]{:S(2)}) collective-permute-start(f32[8,2,130,1]{2,0,3,1:T(8,128)S(1)} %copy.105), channel_id=1, source_target_pairs={{0,1},{1,2},{2,3},{3,4},{4,5},{5,6},{6,7},{7,8},{8,9},{9,10},{10,1... | collective-permute-start | bytes 24968 | tf_op jit(solution)/shard_map/ppermute | solution.py:23
  140.7 1.2 copy-start.5
  143.0 1.8 copy-start.6
  143.0 1.8 copy-start.7
  219.4 23.0 %copy-start.11 = (f32[4096]{0:T(1024)S(1)}, f32[4096]{0:T(1024)}, u32[]{:S(2)}) copy-start(f32[4096]{0:T(1024)} %gather_fusion.3) | copy-start | bytes 49156
  278.9 10.7 %copy-start.4 = (f32[3,1,128,128]{3,2,1,0:T(8,128)S(1)}, f32[3,1,128,128]{3,2,1,0:T(8,128)}, u32[]{:S(2)}) copy-start(f32[3,1,128,128]{3,2,1,0:T(8,128)} %get-tuple-element.112) | copy-start | bytes 589828
  377.7 50.7 %copy-start.3 = (bf16[32,128,128]{2,1,0:T(8,128)(2,1)S(1)}, bf16[32,128,128]{2,1,0:T(8,128)(2,1)}, u32[]{:S(2)}) copy-start(bf16[32,128,128]{2,1,0:T(8,128)(2,1)} %minimum_convert_fusion) | copy-start | bytes 3145732
  377.7 52.5 %copy-start.10 = (f32[4096]{0:T(1024)S(1)}, f32[4096]{0:T(1024)}, u32[]{:S(2)}) copy-start(f32[4096]{0:T(1024)} %gather_fusion.5) | copy-start | bytes 49156
  382.3 49.8 %copy-start.14 = (f32[32]{0:T(128)S(1)}, f32[32]{0:T(128)}, u32[]{:S(2)}) copy-start(f32[32]{0:T(128)} %slice_reduce_fusion.2) | copy-start | bytes 388
  382.3 49.8 %copy-start.15 = (s32[32]{0:T(128)S(1)}, s32[32]{0:T(128)}, u32[]{:S(2)}) copy-start(s32[32]{0:T(128)} %param.33) | copy-start | bytes 388
  382.3 49.8 %copy-start.17 = (f32[32]{0:T(128)S(1)}, f32[32]{0:T(128)}, u32[]{:S(2)}) copy-start(f32[32]{0:T(128)} %param.35) | copy-start | bytes 388
  382.3 49.8 %copy-start.18 = (f32[32]{0:T(128)S(1)}, f32[32]{0:T(128)}, u32[]{:S(2)}) copy-start(f32[32]{0:T(128)} %param.34) | copy-start | bytes 388
  382.4 49.8 %copy-start.20 = (s32[32,1]{0,1:T(1,128)S(1)}, s32[32,1]{0,1:T(1,128)}, u32[]{:S(2)}) copy-start(s32[32,1]{0,1:T(1,128)} %param.36) | copy-start | bytes 388
  382.4 49.8 %copy-start.21 = (f32[32]{0:T(128)S(1)}, f32[32]{0:T(128)}, u32[]{:S(2)}) copy-start(f32[32]{0:T(128)} %convolution_bitcast_fusion) | copy-start | bytes 388
  382.4 50.1 %copy-start.13 = (f32[32,128]{1,0:T(8,128)S(1)}, f32[32,128]{1,0:T(8,128)}, u32[]{:S(2)}) copy-start(f32[32,128]{1,0:T(8,128)} %param.32) | copy-start | bytes 49156
where the time goes:
time: 512 us; the launch traced here: 511 us
  local copies, waits for them, and re-layouts  233 us (46%)
  blocking collectives  154 us (30%)
  other arithmetic  93.7 us (18%)
  starting transfers between devices  19.4 us (4%)
  matrix products  9.4 us (2%)
    psum x1, blocking collectives, per_device(): group_rates = lax.psum(rates_part, ('gx', 'gy'))  75.3 us
    scatter-add x2, other arithmetic, local_terms(): residual = residual.reshape(3, -1).at[:, flat_cell.reshape(-1)].add(rates...  73.5 us
    gather x2, local copies, waits for them, and re-layouts, equations(): above = jnp.take_along_axis(seg_vals, parent, axis=1)  68.8 us
    gather x2, local copies, waits for them, and re-layouts, local_terms(): press_in.reshape(-1)[flat_cell] - seg_vals  63.6 us
    psum x1, blocking collectives, per_device(): total_sum, tangent_sum = lax.psum((rate_total, total_tangent), 'gy')  46 us
    gather x2, local copies, waits for them, and re-layouts, local_terms(): mobil_flat[:, flat_cell]  36.5 us
    psum x1, blocking collectives, per_device(): guide_total = lax.psum(guide_part, 'gx')  32.3 us
    unnamed x49, local copies, waits for them, and re-layouts  24.4 us
  transfers between devices with their start and end apart: 4, of which 0 were waited for; matrix products, arithmetic and copies ran while one was open for 15% of the time, Pallas kernels for 0%

commit v1 on v0

--- a/solution.py
+++ b/solution.py
@@ -11,6 +11,14 @@
 UPWIND_WIDTH = 0.02
 FRICTION = 0.002
 RATE_SCALE = 0.1
+
+
+def added_up(shard, axis):
+    size, total = (lax.axis_size(axis), shard)
+    for stride in [1 << k for k in range(size.bit_length() - 1)]:
+        route = [(i, i ^ stride) for i in range(size)]
+        total = total + lax.ppermute(total, axis, route)
+    return total
 
 
 def padded_2(x, sides, width):
@@ -184,7 +192,7 @@
     ).astype(jnp.float32)
     rates_part = jnp.dot(jnp.sum(rates, axis=2), member, precision=lax.Precision.HIGHEST)
     guide_part = jnp.dot(guide_rate, member, precision=lax.Precision.HIGHEST)
-    guide_total = lax.psum(guide_part, "gx")
+    guide_total = added_up(guide_part, "gx")
     group_rates = lax.psum(rates_part, ("gx", "gy"))
     target = (
         jnp.dot(member, group_target, precision=lax.Precision.HIGHEST)

time: 512 us -> 485 us (0.947)
  blocking collectives: 154 us -> 122 us
    psum x1 -> x0, blocking collectives: 32.3 us -> none  [per_device(): guide_total = lax.psum(guide_part, 'gx')]
    gather x2, local copies, waits for them, and re-layouts: 63.6 us -> 46.1 us  [local_terms(): press_in.reshape(-1)[flat_cell] - seg_vals]
    gather x2, local copies, waits for them, and re-layouts: 68.8 us -> 86.3 us  [equations(): above = jnp.take_along_axis(seg_vals, parent, axis=1)]
    ppermute x0 -> x4, starting transfers between devices: none -> 9.12 us  [added_up(): total = total + lax.ppermute(total, axis, route)]
    ppermute x2, starting transfers between devices: 11.2 us -> 5 us  [padded_2(): after = lax.ppermute(first, axis, down)]
    unnamed x49 -> x55, local copies, waits for them, and re-layouts: 24.4 us -> 24.4 us
  transfers between devices with their start and end apart: 4 -> 8, of which waited for: 0 -> 0; matrix products, arithmetic and copies ran while one was open for 15% -> 68% of each run, Pallas kernels for 0% -> 0%
where the time goes in v1:
time: 485 us; the launch traced here: 484 us
  local copies, waits for them, and re-layouts  232 us (48%)
  blocking collectives  122 us (25%)
  other arithmetic  94.2 us (19%)
  starting transfers between devices  22.1 us (5%)
  matrix products  11.6 us (2%)
    gather x2, local copies, waits for them, and re-layouts, equations(): above = jnp.take_along_axis(seg_vals, parent, axis=1)  86.3 us
    psum x1, blocking collectives, per_device(): group_rates = lax.psum(rates_part, ('gx', 'gy'))  76.2 us
    scatter-add x2, other arithmetic, local_terms(): residual = residual.reshape(3, -1).at[:, flat_cell.reshape(-1)].add(rates...  73.5 us
    gather x2, local copies, waits for them, and re-layouts, local_terms(): press_in.reshape(-1)[flat_cell] - seg_vals  46.1 us
    psum x1, blocking collectives, per_device(): total_sum, tangent_sum = lax.psum((rate_total, total_tangent), 'gy')  45.8 us
    gather x2, local copies, waits for them, and re-layouts, local_terms(): mobil_flat[:, flat_cell]  36.5 us
    unnamed x55, local copies, waits for them, and re-layouts  24.4 us
    slice x2, local copies, waits for them, and re-layouts, local_terms(): mobil_in = mobility[:, :, 1:-1, 1:-1]  17.2 us
  transfers between devices with their start and end apart: 8, of which 0 were waited for; matrix products, arithmetic and copies ran while one was open for 68% of the time, Pallas kernels for 0%

profile of v1, /device:TPU:1, one launch (start us, length us, event | category | flops | bytes accessed | tf_op | source)
XLA Modules:
  0.0 483.5 jit_solution(9208708360591758359)
XLA Ops:
  0.7 0.9 bitcast_dynamic-update-slice_fusion
  1.7 1.0 constant_dynamic-update-slice_fusion.1
  2.7 1.0 constant_dynamic-update-slice_fusion
  3.7 1.0 select_dynamic-update-slice_fusion.1
  4.7 0.9 select_dynamic-update-slice_fusion
  5.6 1.3 collective-permute-start.1
  6.9 4.6 collective-permute-start
  11.7 1.5 collective-permute-start.4
  13.3 0.6 compare_select_fusion
  13.9 0.8 minimum_convert_fusion.6
  14.7 1.0 minimum_convert_fusion.4
  15.7 1.0 minimum_convert_fusion.2
  16.7 2.0 minimum_convert_fusion
  18.7 0.7 fusion.14
  19.5 4.6 collective-permute-start.5
  24.3 0.4 fusion.171
  24.6 0.6 copy.106
  25.2 3.7 collective-permute-start.3
  29.0 0.6 copy.105
  29.6 3.5 collective-permute-start.2
  33.1 43.2 %gather_fusion.5 = f32[4096]{0:T(1024)} fusion(f32[32,128]{1,0:T(8,128)S(1)} %copy-done.2, s32[4096]{0:T(1024)S(1)} %fusion.156), kind=kCustom, calls=%fused_computation.5 | custom fusion | bytes 65536 | tf_op jit(solution)/shard_map/jvp(jit(take_along_axis))/gather | solution.py:79
  76.3 1.4 collective-permute-start.6
  77.7 43.1 %gather_fusion.4 = f32[4096]{0:T(1024)} fusion(f32[32,128]{1,0:T(8,128)S(1)} %copy-done.3, s32[4096]{0:T(1024)S(1)} %fusion.156), kind=kCustom, calls=%fused_computation.4 | custom fusion | bytes 65536 | tf_op jit(solution)/shard_map/jvp(jit(take_along_axis))/gather | solution.py:79
  120.9 0.6 compare_reduce_fusion
  121.5 0.5 add.280
  122.0 1.6 collective-permute-start.7
  123.7 0.4 copy.108
  124.1 0.4 copy.107
  124.5 1.0 pad_maximum_fusion
  125.6 0.3 fusion.38
  126.0 1.2 fusion.39
  127.3 0.5 fusion.54
  127.8 0.4 fusion.89
  128.7 0.7 fusion.60
  129.4 0.5 fusion.95
  130.5 0.3 pad_maximum_fusion.6
  131.0 1.0 pad_maximum_fusion.2
  132.1 0.8 pad_maximum_fusion.4
  132.9 0.7 pad_maximum_fusion.14
  133.6 0.3 fusion.34
  134.0 8.6 %copy.109 = f32[3,2,128,128]{0,3,2,1:T(8,128)} copy(f32[3,2,128,128]{3,2,1,0:T(8,128)S(1)} %fusion.34) | data formatting | bytes 786432 | tf_op jit(solution)/shard_map/jvp()/sub | solution.py:171
  142.6 8.6 %copy.110 = f32[3,2,128,128]{0,3,2,1:T(8,128)} copy(f32[3,2,128,128]{3,2,1,0:T(8,128)S(1)} %get-tuple-element.106) | data formatting | bytes 786432 | tf_op jit(solution)/shard_map/jvp()/slice | solution.py:141
  151.2 16.5 %gather_fusion = f32[4096,3]{1,0:T(8,128)S(1)} fusion(f32[3,32768]{0,1:T(8,128)} %bitcast.414, s32[4096]{0:T(1024)S(1)} %get-tuple-element.69), kind=kCustom, calls=%fused_computation | custom fusion | bytes 114688 | tf_op jit(solution)/shard_map/jvp()/gather | solution.py:176
  167.7 23.0 %gather_fusion.3 = f32[4096]{0:T(1024)S(1)} fusion(f32[32768]{0:T(1024)S(1)} %bitcast.407, s32[4096]{0:T(1024)S(1)} %get-tuple-element.69), kind=kCustom, calls=%fused_computation.3 | custom fusion | bytes 49152 | tf_op jit(solution)/shard_map/jvp()/gather | solution.py:176
  190.8 23.0 %gather_fusion.1 = f32[4096]{0:T(1024)S(1)} fusion(f32[32768]{0:T(1024)S(1)} %bitcast.408, s32[4096]{0:T(1024)S(1)} %get-tuple-element.69), kind=kCustom, calls=%fused_computation.1 | custom fusion | bytes 49152 | tf_op jit(solution)/shard_map/jvp()/gather | solution.py:176
  213.8 8.6 %copy.112 = f32[3,2,128,128]{0,3,2,1:T(8,128)} copy(f32[3,2,128,128]{3,2,1,0:T(8,128)S(1)} %get-tuple-element.105) | data formatting | bytes 786432 | tf_op jit(solution)/shard_map/jvp()/slice | solution.py:141
  222.4 19.9 %gather_fusion.2 = f32[4096,3]{1,0:T(8,128)} fusion(f32[3,32768]{0,1:T(8,128)} %bitcast.415, s32[4096]{0:T(1024)S(1)} %get-tuple-element.69), kind=kCustom, calls=%fused_computation.2 | custom fusion | bytes 114688 | tf_op jit(solution)/shard_map/jvp()/gather | solution.py:176
  242.4 5.2 %add_reduce_fusion = (f32[32,128]{1,0:T(8,128)S(1)}, f32[32,128]{1,0:T(8,128)S(1)}, f32[3,32]{0,1:T(8,128)}) fusion(f32[3,32,128]{0,2,1:T(8,128)} %bitcast.416, f32[3,32,128]{0,2,1:T(8,128)S(1)} %bitcast.413, f32[32,128]{1,0:T(8,128)S(1)} %get-tuple-element.113, f32[32,128]{1,0:T(8,128)S(1)} %get-tuple-element.114, f32[32,128]{1,0:T(8,128)S(1)} %and_select_fusion, ...), kind=kLoop, calls=%fused_computation.17 | loop fusion | flops 126880 | bytes 229760 | tf_op jit(solution)/shard_map/reduce_sum | solution.py:189
  247.6 45.8 %all-reduce.4 = (f32[32,128]{1,0:T(8,128)}, f32[32,128]{1,0:T(8,128)}) all-reduce(f32[32,128]{1,0:T(8,128)S(1)} %get-tuple-element.55, f32[32,128]{1,0:T(8,128)S(1)} %get-tuple-element.54), channel_id=1, replica_groups=mesh['gx'=16,'gy'=16] {'gy'}, use_global_device_ids=true, to_apply=%region_3.4 | all-reduce | flops 8192 | bytes 65536 | tf_op jit(solution)/shard_map/psum | solution.py:209
  293.4 2.6 fusion.174
  296.1 0.8 fusion.152
  296.9 2.4 fusion.173
  299.5 0.3 fusion.31
  299.8 36.5 %scatter_custom_fusion = f32[3,32768]{0,1:T(8,128)} fusion(f32[3,32768]{0,1:T(8,128)} %bitcast.409, s32[4096]{0:T(1024)} %bitcast.429, f32[4096,3]{1,0:T(8,128)S(1)} %gather_fusion, f32[4096]{0:T(1024)S(1)} %bitcast.419, f32[4096]{0:T(1024)S(1)} %bitcast.417), kind=kCustom, calls=%fused_computation.15 | custom fusion | flops 36864 | bytes 475136 | tf_op jit(solution)/shard_map/jvp()/scatter-add | solution.py:180
  336.3 10.6 %copy.115 = f32[3,2,128,128]{3,2,1,0:T(8,128)} copy(f32[3,2,128,128]{0,3,2,1:T(8,128)} %bitcast.410) | data formatting | bytes 786432
  346.9 8.6 %copy.111 = f32[3,2,128,128]{0,3,2,1:T(8,128)} copy(f32[3,2,128,128]{3,2,1,0:T(8,128)S(1)} %fusion.31) | data formatting | bytes 786432 | tf_op jit(solution)/shard_map/jvp()/sub | solution.py:171
  355.5 37.0 %scatter_custom_fusion.1 = f32[3,32768]{0,1:T(8,128)} fusion(f32[3,32768]{0,1:T(8,128)} %bitcast.411, s32[4096]{0:T(1024)} %bitcast.430, f32[4096,3]{1,0:T(8,128)} %gather_fusion.2, f32[4096,3]{1,0:T(8,128)S(1)} %gather_fusion, f32[4096]{0:T(1024)S(1)} %bitcast.425, f32[4096]{0:T(1024)S(1)} %bitcast.420, f32[4096]{0:T(1024)S(1)} %bitcast.418), kind=kCustom, calls=%fused_computation.13 | custom fusion | flops 73728 | bytes 2588672 | tf_op jit(solution)/shard_map/jvp()/scatter-add | solution.py:180
  392.6 10.7 %copy.116 = f32[3,2,128,128]{3,2,1,0:T(8,128)} copy(f32[3,2,128,128]{0,3,2,1:T(8,128)} %bitcast.412) | data formatting | bytes 786432
  403.3 0.8 fusion.19
  404.3 0.7 slice_select_fusion.1
  405.1 0.6 slice_select_fusion
  405.9 0.6 constant_dynamic-slice_fusion.1
  406.5 0.6 constant_dynamic-slice_fusion
  407.3 76.2 %psum.23 = f32[3,128]{1,0:T(4,128)} all-reduce(f32[3,128]{1,0:T(4,128)S(1)} %fusion.157), channel_id=1, replica_groups=mesh['gx'=16,'gy'=16] {'gx','gy'}, use_global_device_ids=true, to_apply=%region_8.9 | all-reduce | flops 384 | bytes 3072 | tf_op jit(solution)/shard_map/psum | solution.py:196
  (89 shorter events, 3.2 us)
Async XLA Ops:
  0.6 18.0 %copy-start = (f32[128]{0:T(128)S(1)}, f32[128]{0:T(128)}, u32[]{:S(2)}) copy-start(f32[128]{0:T(128)} %param.37) | copy-start | bytes 1540
  0.7 10.9 %copy-start.21 = (f32[32]{0:T(128)S(1)}, f32[32]{0:T(128)}, u32[]{:S(2)}) copy-start(f32[32]{0:T(128)} %param.35) | copy-start | bytes 388
  0.7 10.9 %copy-start.23 = (s32[32,1]{0,1:T(1,128)S(1)}, s32[32,1]{0,1:T(1,128)}, u32[]{:S(2)}) copy-start(s32[32,1]{0,1:T(1,128)} %param.36) | copy-start | bytes 388
  0.7 12.5 %copy-start.14 = (s32[32,128]{1,0:T(8,128)S(1)}, s32[32,128]{1,0:T(8,128)}, u32[]{:S(2)}) copy-start(s32[32,128]{1,0:T(8,128)} %param.29) | copy-start | bytes 49156
  0.7 13.2 %copy-start.18 = (f32[32,128]{1,0:T(8,128)S(1)}, f32[32,128]{1,0:T(8,128)}, u32[]{:S(2)}) copy-start(f32[32,128]{1,0:T(8,128)} %param.30) | copy-start | bytes 49156
  0.7 13.2 %copy-start.15 = (s32[32,128]{1,0:T(8,128)S(1)}, s32[32,128]{1,0:T(8,128)}, u32[]{:S(2)}) copy-start(s32[32,128]{1,0:T(8,128)} %param.31) | copy-start | bytes 49156
  5.6 18.5 %collective-permute-start.1 = (f32[8,2,1,128]{3,2,1,0:T(1,128)S(1)}, f32[8,2,1,128]{3,2,1,0:T(1,128)S(1)}, u32[]{:S(2)}, u32[]{:S(2)}) collective-permute-start(f32[8,2,1,128]{3,2,1,0:T(1,128)S(1)} %get-tuple-element.89), channel_id=1, source_target_pairs={{16,0},{32,16},{48,32},{64,48},{80,64},{96,80},{112,96},{128,112},... | collective-permute-start | bytes 24584 | tf_op jit(solution)/shard_map/ppermute | solution.py:32
  6.9 17.2 %collective-permute-start = (f32[8,2,1,128]{3,2,1,0:T(1,128)S(1)}, f32[8,2,1,128]{3,2,1,0:T(1,128)S(1)}, u32[]{:S(2)}, u32[]{:S(2)}) collective-permute-start(f32[8,2,1,128]{3,2,1,0:T(1,128)S(1)} %get-tuple-element.88), channel_id=1, source_target_pairs={{0,16},{16,32},{32,48},{48,64},{64,80},{80,96},{96,112},{112,128},... | collective-permute-start | bytes 24584 | tf_op jit(solution)/shard_map/ppermute | solution.py:31
  11.7 7.8 %collective-permute-start.4 = (f32[128]{0:T(128)S(1)}, f32[128]{0:T(128)S(1)}, u32[]{:S(2)}, u32[]{:S(2)}) collective-permute-start(f32[128]{0:T(128)S(1)} %convolution_bitcast_fusion.1), channel_id=1, source_target_pairs={{0,16},{16,0},{32,48},{48,32},{64,80},{80,64},{96,112},{112,96},{1... | collective-permute-start | bytes 1544 | tf_op jit(solution)/shard_map/ppermute | solution.py:20
  16.7 2.7 copy-start.3
  19.5 56.8 %collective-permute-start.5 = (f32[128]{0:T(128)S(1)}, f32[128]{0:T(128)S(1)}, u32[]{:S(2)}, u32[]{:S(2)}) collective-permute-start(f32[128]{0:T(128)S(1)} %add.278), channel_id=1, source_target_pairs={{0,32},{16,48},{32,0},{48,16},{64,96},{80,112},{96,64},{112,80},{1... | collective-permute-start | bytes 1544 | tf_op jit(solution)/shard_map/ppermute | solution.py:20
  24.6 8.4 %copy-start.2 = (f32[32,128]{1,0:T(8,128)S(1)}, f32[32,128]{1,0:T(8,128)}, u32[]{:S(2)}) copy-start(f32[32,128]{1,0:T(8,128)} %param.28) | copy-start | bytes 49156
  25.2 98.4 %collective-permute-start.3 = (f32[8,2,130,1]{2,0,3,1:T(8,128)S(1)}, f32[8,2,130,1]{2,0,3,1:T(8,128)S(1)}, u32[]{:S(2)}, u32[]{:S(2)}) collective-permute-start(f32[8,2,130,1]{2,0,3,1:T(8,128)S(1)} %copy.106), channel_id=1, source_target_pairs={{1,0},{2,1},{3,2},{4,3},{5,4},{6,5},{7,6},{8,7},{9,8},{10,9},{11,1... | collective-permute-start | bytes 24968 | tf_op jit(solution)/shard_map/ppermute | solution.py:32
  29.6 94.5 %collective-permute-start.2 = (f32[8,2,130,1]{2,0,3,1:T(8,128)S(1)}, f32[8,2,130,1]{2,0,3,1:T(8,128)S(1)}, u32[]{:S(2)}, u32[]{:S(2)}) collective-permute-start(f32[8,2,130,1]{2,0,3,1:T(8,128)S(1)} %copy.105), channel_id=1, source_target_pairs={{0,1},{1,2},{2,3},{3,4},{4,5},{5,6},{6,7},{7,8},{8,9},{9,10},{10,1... | collective-permute-start | bytes 24968 | tf_op jit(solution)/shard_map/ppermute | solution.py:31
  76.3 45.2 %collective-permute-start.6 = (f32[128]{0:T(128)S(1)}, f32[128]{0:T(128)S(1)}, u32[]{:S(2)}, u32[]{:S(2)}) collective-permute-start(f32[128]{0:T(128)S(1)} %add.279), channel_id=1, source_target_pairs={{0,64},{16,80},{32,96},{48,112},{64,0},{80,16},{96,32},{112,48},{1... | collective-permute-start | bytes 1544 | tf_op jit(solution)/shard_map/ppermute | solution.py:20
  122.0 281.2 %collective-permute-start.7 = (f32[128]{0:T(128)}, f32[128]{0:T(128)}, u32[]{:S(2)}, u32[]{:S(2)}) collective-permute-start(f32[128]{0:T(128)} %add.280), channel_id=1, source_target_pairs={{0,128},{16,144},{32,160},{48,176},{64,192},{80,208},{96,224},{112... | collective-permute-start | bytes 1544 | tf_op jit(solution)/shard_map/ppermute | solution.py:20
  128.7 1.2 copy-start.10
  131.0 2.6 copy-start.11
  131.0 2.6 copy-start.13
  242.4 51.1 %copy-start.4 = (bf16[32,128,128]{2,1,0:T(8,128)(2,1)S(1)}, bf16[32,128,128]{2,1,0:T(8,128)(2,1)}, u32[]{:S(2)}) copy-start(bf16[32,128,128]{2,1,0:T(8,128)(2,1)} %minimum_convert_fusion) | copy-start | bytes 3145732
  293.4 6.1 %copy-start.5 = (f32[3,2,129,128]{3,2,1,0:T(8,128)S(1)}, f32[3,2,129,128]{3,2,1,0:T(8,128)}, u32[]{:S(2)}) copy-start(f32[3,2,129,128]{3,2,1,0:T(8,128)} %get-tuple-element.110) | copy-start | bytes 1188868
  293.4 6.1 %copy-start.6 = (f32[3,2,128,129]{3,2,1,0:T(8,128)S(1)}, f32[3,2,128,129]{3,2,1,0:T(8,128)}, u32[]{:S(2)}) copy-start(f32[3,2,128,129]{3,2,1,0:T(8,128)} %get-tuple-element.108) | copy-start | bytes 1188868
  293.4 6.1 %copy-start.7 = (f32[1,2,130,130]{3,2,1,0:T(8,128)S(1)}, f32[1,2,130,130]{3,2,1,0:T(8,128)}, u32[]{:S(2)}) copy-start(f32[1,2,130,130]{3,2,1,0:T(8,128)} %get-tuple-element.74) | copy-start | bytes 405604
  293.4 6.1 %copy-start.8 = (f32[1,2,130,130]{3,2,1,0:T(8,128)S(1)}, f32[1,2,130,130]{3,2,1,0:T(8,128)}, u32[]{:S(2)}) copy-start(f32[1,2,130,130]{3,2,1,0:T(8,128)} %get-tuple-element.75) | copy-start | bytes 405604
  293.4 6.1 %copy-start.9 = (f32[3,1,128,128]{3,2,1,0:T(8,128)S(1)}, f32[3,1,128,128]{3,2,1,0:T(8,128)}, u32[]{:S(2)}) copy-start(f32[3,1,128,128]{3,2,1,0:T(8,128)} %get-tuple-element.112) | copy-start | bytes 589828
  293.4 6.1 %copy-start.12 = (f32[2,128,128]{2,1,0:T(8,128)S(1)}, f32[2,128,128]{2,1,0:T(8,128)}, u32[]{:S(2)}) copy-start(f32[2,128,128]{2,1,0:T(8,128)} %param.24) | copy-start | bytes 393220
  392.5 10.8 %copy-start.20 = (s32[32]{0:T(128)S(1)}, s32[32]{0:T(128)}, u32[]{:S(2)}) copy-start(s32[32]{0:T(128)} %param.33) | copy-start | bytes 388
  392.5 10.8 %copy-start.22 = (f32[32]{0:T(128)S(1)}, f32[32]{0:T(128)}, u32[]{:S(2)}) copy-start(f32[32]{0:T(128)} %param.34) | copy-start | bytes 388
  392.5 10.8 %copy-start.24 = (f32[32]{0:T(128)S(1)}, f32[32]{0:T(128)}, u32[]{:S(2)}) copy-start(f32[32]{0:T(128)} %fusion.14) | copy-start | bytes 388
  392.5 11.7 %copy-start.16 = (f32[4096]{0:T(1024)S(1)}, f32[4096]{0:T(1024)}, u32[]{:S(2)}) copy-start(f32[4096]{0:T(1024)} %gather_fusion.4) | copy-start | bytes 49156
  392.5 11.7 %copy-start.19 = (f32[32,128]{1,0:T(8,128)S(1)}, f32[32,128]{1,0:T(8,128)}, u32[]{:S(2)}) copy-start(f32[32,128]{1,0:T(8,128)} %param.32) | copy-start | bytes 49156
  392.5 14.5 %copy-start.17 = (f32[3,32]{0,1:T(8,128)S(1)}, f32[3,32]{0,1:T(8,128)}, u32[]{:S(2)}) copy-start(f32[3,32]{0,1:T(8,128)} %get-tuple-element.56) | copy-start | bytes 1156
  392.5 91.0 %copy-start.1 = (f32[128]{0:T(128)S(1)}, f32[128]{0:T(128)}, u32[]{:S(2)}) copy-start(f32[128]{0:T(128)} %param.37) | copy-start | bytes 1540
